TPU v7x, 32 devices: a whole 2x2x4 slice. The times are simulated.
32 devices in a mesh: gx: 4 (over z), gy: 8 (over y, x, core).
Axes of the slice: x: 2, y: 2, z: 4, core: 2. Of those that a mesh axis runs over, the one named last changes fastest.
Arguments:
- seismic: float32 [512, 512, 256], P('gx', 'gy'), may hold values from -41 to 41, as said below
Outputs:
- shift_field: float32 [512, 512, 256], P('gx', 'gy')
- residual: float32 [512, 512, 256], P('gx', 'gy')
Inputs may be any that keep to these rules, and one draw needn't show every extreme that they name: `seismic`: recorded amplitudes of the window.
All inputs are finite; a program needn't handle non-finite values.
Results may differ from a plain program's by a relative error of at most 0.0003.
Values sent between devices are 32-bit elements; how exact they have to be, the bound alone decides.
A program may use at most 320 MiB of HBM per device.

v0:
```python
import jax
import jax.numpy as jnp
from jax import lax
from jax.sharding import PartitionSpec as P

NX = 512
NY = 512
ITERS = 2
damping = 0.001
floor_term = 0.5
highest = lax.Precision.HIGHEST


def extended(block, sides, width):
    for axis, dim in sides:
        count = lax.axis_size(axis)
        forward = [(i, i + 1) for i in range(count - 1)]
        backward = [(target, source) for source, target in forward]
        low = lax.ppermute(
            lax.slice_in_dim(block, block.shape[dim] - width, None, axis=dim), axis, forward
        )
        high = lax.ppermute(lax.slice_in_dim(block, 0, width, axis=dim), axis, backward)
        block = jnp.concatenate([low, block, high], axis=dim)
    return block


def cut(field, start, stop, axis):
    return lax.slice_in_dim(field, start, stop, axis=axis)


def smooth_axis(field, axis):
    length = field.shape[axis]
    return 0.25 * (
        cut(field, 0, length - 2, axis)
        + 2.0 * cut(field, 1, length - 1, axis)
        + cut(field, 2, length, axis)
    )


def pad_time(field):
    return jnp.pad(field, ((0, 0), (0, 0), (1, 1)))


def smooth_all(field):
    return smooth_axis(pad_time(smooth_axis(smooth_axis(field, 0), 1)), 2)


def tensor_fields(padded, inside_x, inside_y):
    mask = inside_x[:, None, None] * inside_y[None, :, None]
    grad_x = 0.5 * (padded[2:, 1:-1] - padded[:-2, 1:-1]) * mask
    grad_y = 0.5 * (padded[1:-1, 2:] - padded[1:-1, :-2]) * mask
    timed = pad_time(padded[1:-1, 1:-1])
    grad_t = 0.5 * (timed[:, :, 2:] - timed[:, :, :-2]) * mask
    cross_x = smooth_all(grad_x * grad_t)
    cross_y = smooth_all(grad_y * grad_t)
    along_t = smooth_all(grad_t * grad_t) + floor_term
    spread = smooth_all(grad_x * grad_x + grad_y * grad_y)
    return (-cross_x / along_t, -cross_y / along_t, along_t / (along_t + spread))


def cosine_table(order):
    freq = jnp.arange(order, dtype=jnp.float32)[:, None]
    place = jnp.arange(order, dtype=jnp.float32)[None, :]
    scale = jnp.where(freq == 0.0, jnp.sqrt(1.0 / order), jnp.sqrt(2.0 / order)).astype(jnp.float32)
    return scale * jnp.cos(jnp.pi * (place + 0.5) * freq / order)


def eigen_values(order):
    freq = jnp.arange(order, dtype=jnp.float32)
    return 2.0 - 2.0 * jnp.cos(jnp.pi * freq / order)


def combine_terms(field, upper_x, lower_x, upper_y, lower_y, weight_x, weight_y, prior_x, prior_y):
    return (
        damping * field
        + weight_x * (field - upper_x)
        + prior_x * (field - lower_x)
        + weight_y * (field - upper_y)
        + prior_y * (field - lower_y)
    )


def operate(field, weight_x, weight_y, prior_x, prior_y):
    padded = extended(field, (("gx", 0), ("gy", 1)), 1)
    return combine_terms(
        field,
        padded[2:, 1:-1],
        padded[:-2, 1:-1],
        padded[1:-1, 2:],
        padded[1:-1, :-2],
        weight_x,
        weight_y,
        prior_x,
        prior_y,
    )


def solve_front(front, table_x, table_y, plane_denom):
    hat = jnp.einsum("ki,tij->tkj", table_x, front, precision=highest)
    hat = jnp.einsum("lj,tkj->tkl", table_y, hat, precision=highest)
    hat = hat / plane_denom
    hat = jnp.einsum("lj,tkl->tkj", table_y, hat, precision=highest)
    return jnp.einsum("ki,tkj->tij", table_x, hat, precision=highest)


def slice_solve(whole, table_x, table_y, plane_denom):
    front = jnp.transpose(whole, (2, 0, 1))
    return jnp.transpose(solve_front(front, table_x, table_y, plane_denom), (1, 2, 0))


def reorder_back(back, rows_x, rows_y, parts_x, parts_y, depth):
    per = depth // (parts_x * parts_y)
    target = jnp.arange(depth, dtype=jnp.int32)
    outer = target // (parts_y * per)
    middle = target // per % parts_y
    source = middle * (parts_x * per) + outer * per + target % per
    select = (jnp.arange(depth, dtype=jnp.int32)[:, None] == source[None, :]).astype(jnp.float32)
    flat = back.reshape(rows_x * rows_y, depth)
    return jnp.dot(flat, select, precision=highest, preferred_element_type=jnp.float32).reshape(
        rows_x, rows_y, depth
    )


def inner(first, second):
    return lax.psum(jnp.sum(first * second), ("gx", "gy"))


def solve(rhs, apply_op, precondition):
    shift_field = jnp.zeros_like(rhs)
    residual = rhs
    precond = precondition(residual)
    direction = precond
    norm_now = inner(residual, precond)
    for step in range(ITERS):
        image = apply_op(direction)
        alpha = norm_now / lax.psum(jnp.sum(direction * image), ("gx", "gy"))
        shift_field = shift_field + alpha * direction
        residual = residual - alpha * image
        if step + 1 < ITERS:
            precond = precondition(residual)
            norm_next = inner(residual, precond)
            direction = precond + norm_next / norm_now * direction
            norm_now = norm_next
    return (shift_field, residual)


def per_device(seismic):
    rows_x, rows_y, depth = seismic.shape
    parts_x = lax.axis_size("gx")
    parts_y = lax.axis_size("gy")
    base_x = lax.axis_index("gx") * rows_x
    base_y = lax.axis_index("gy") * rows_y
    table_x = cosine_table(NX)
    table_y = cosine_table(NY)
    eigen_x = eigen_values(NX)
    eigen_y = eigen_values(NY)
    plane_denom = damping + eigen_x[:, None] + eigen_y[None, :]
    padded = extended(seismic, (("gx", 0), ("gy", 1)), 3)
    grid_x = base_x + jnp.arange(-2, rows_x + 2, dtype=jnp.int32)
    grid_y = base_y + jnp.arange(-2, rows_y + 2, dtype=jnp.int32)
    inside_x = ((grid_x >= 0) & (grid_x < NX)).astype(jnp.float32)
    inside_y = ((grid_y >= 0) & (grid_y < NY)).astype(jnp.float32)
    dip_x, dip_y, weight = tensor_fields(padded, inside_x, inside_y)
    edge_x = grid_x[1:-1]
    edge_y = grid_y[1:-1]
    keep_x = ((edge_x >= 0) & (edge_x < NX - 1)).astype(jnp.float32)
    keep_y = ((edge_y >= 0) & (edge_y < NY - 1)).astype(jnp.float32)
    weight_x = weight * keep_x[:, None, None]
    weight_y = weight * keep_y[None, :, None]
    flux_x = weight_x * dip_x
    flux_y = weight_y * dip_y
    rhs = flux_x[:-2, 1:-1] - flux_x[1:-1, 1:-1] + (flux_y[1:-1, :-2] - flux_y[1:-1, 1:-1])
    own_x = weight_x[1:-1, 1:-1]
    prior_x = weight_x[:-2, 1:-1]
    own_y = weight_y[1:-1, 1:-1]
    prior_y = weight_y[1:-1, :-2]

    def precondition(field):
        whole = lax.all_to_all(
            lax.all_to_all(field, "gx", split_axis=2, concat_axis=0, tiled=True),
            "gy",
            split_axis=2,
            concat_axis=1,
            tiled=True,
        )
        hat = slice_solve(whole, table_x, table_y, plane_denom)
        back = lax.all_to_all(
            lax.all_to_all(hat, "gx", split_axis=0, concat_axis=2, tiled=True),
            "gy",
            split_axis=1,
            concat_axis=2,
            tiled=True,
        )
        return reorder_back(back, rows_x, rows_y, parts_x, parts_y, depth)

    def apply_tiles(field):
        return operate(field, own_x, own_y, prior_x, prior_y)

    return solve(rhs, apply_tiles, precondition)


def solution(mesh):
    placed = (P("gx", "gy", None),)
    return jax.shard_map(
        per_device,
        mesh=mesh,
        in_specs=placed,
        out_specs=(P("gx", "gy", None), P("gx", "gy", None)),
        check_vma=False,
    )
```

profile of v0, /device:TPU:0, one launch (start us, length us, event | category | flops | bytes accessed | tf_op | source)
XLA Modules:
  0.0 2077.2 jit_solution(1720866723027973175)
XLA Ops:
  47.0 54.0 %fusion.77 = (f32[132,68,256]{2,0,1:T(8,128)}, f32[132,68,256]{2,0,1:T(8,128)}, f32[132,68,256]{2,0,1:T(8,128)}, f32[132,68,256]{2,0,1:T(8,128)}) fusion(f32[132,68]{0,1:T(8,128)S(1)} %multiply_multiply_fusion, f32[134,70,256]{2,0,1:T(8,128)} %copy-done.2, f32[132,68,256]{2,0,1:T(8,128)} %slice.298), kind=kLoop, calls=%fused_computation.146 | loop fusion | flops 36765696 | bytes 82758720 | tf_op jit(solution)/shard_map/mul | solution.py:55
  101.0 29.4 %fusion.6 = (f32[130,68,256]{2,0,1:T(8,128)}, f32[130,68,256]{2,0,1:T(8,128)}) fusion(f32[132,68,256]{2,0,1:T(8,128)} %get-tuple-element.29, f32[132,68,256]{2,0,1:T(8,128)} %get-tuple-element.30), kind=kLoop, calls=%fused_computation.23 | loop fusion | flops 18104320 | bytes 72417280 | tf_op jit(solution)/shard_map/mul | solution.py:33
  150.2 29.4 %fusion.2 = (f32[130,68,256]{2,0,1:T(8,128)}, f32[130,68,256]{2,0,1:T(8,128)}) fusion(f32[132,68,256]{2,0,1:T(8,128)} %get-tuple-element.27, f32[132,68,256]{2,0,1:T(8,128)} %get-tuple-element.28), kind=kLoop, calls=%fused_computation.15 | loop fusion | flops 18104320 | bytes 72417280 | tf_op jit(solution)/shard_map/mul | solution.py:33
  203.3 45.0 %fusion.24 = (f32[130,66,256]{2,0,1:T(8,128)}, f32[130,66,256]{2,0,1:T(8,128)}, f32[130,66,256]{2,0,1:T(8,128)}, f32[130,66,256]{2,0,1:T(8,128)}) fusion(f32[130,66,256]{2,0,1:T(8,128)} %broadcast_multiply_fusion.3, f32[130,68,256]{2,0,1:T(8,128)} %get-tuple-element.46, f32[130]{0:T(256)S(1)} %and_convert_fusion.1, f32[130,68,256]{2,0,1:T(8,128)S(1)} %bitcast.93, ...), kind=kLoop, calls=%fused_computation.47 | loop fusion | flops 61501440 | bytes 140575232 | tf_op jit(solution)/shard_map/mul | solution.py:170
  248.3 26.7 %fusion.30 = (f32[130,66,256]{2,0,1:T(8,128)}, f32[130,66,256]{2,0,1:T(8,128)}) fusion(f32[130,66,256]{2,0,1:T(8,128)} %get-tuple-element.24, f32[130,66,256]{2,0,1:T(8,128)} %broadcast_multiply_fusion.2, f32[130,68,256]{2,0,1:T(8,128)} %get-tuple-element.45, f32[130,66,256]{2,0,1:T(8,128)} %get-tuple-element.23, f32[66]{0:T(128)S(1)} %copy-done.9), kind=kLoop, calls=%fused_computation.53 | loop fusion | flops 24161280 | bytes 70287624 | tf_op jit(solution)/shard_map/mul | solution.py:171
  300.0 185.5 %all_to_all.138 = f32[128,64,256]{0,1,2:T(8,128)S(1)} all-to-all(f32[128,64,256]{0,1,2:T(8,128)} %copy.198), channel_id=1, replica_groups=mesh['gx'=4,'gy'=8] {'gx'}, dimensions={2} | all-to-all | bytes 16777216 | tf_op jit(solution)/shard_map/all_to_all | solution.py:180
  501.6 94.0 %all-to-all-done.1 = f32[512,64,64]{0,1,2:T(8,128)} async-done(((f32[512,64,64]{0,1,2:T(8,128)}), f32[512,64,64]{0,1,2:T(8,128)}, u32[]{:S(2)}, u32[]{:S(2)}) %all-to-all-start.1) | async-done | bytes 8388640 | tf_op jit(solution)/shard_map/all_to_all | solution.py:179
  603.7 22.6 %fusion.66 = f32[8,512,512]{2,1,0:T(8,128)S(1)} fusion(f32[512,512,8]{0,2,1:T(8,128)S(1)} %bitcast.102, f32[512]{0:T(512)S(1)} %get-tuple-element.49, f32[512]{0:T(512)S(1)} %get-tuple-element.50), kind=kOutput, calls=%fused_computation.117 | convolution fusion | flops 12885688320 | bytes 16781312 | tf_op jit(solution)/shard_map/ki,tij->tkj/dot_general | solution.py:99
  626.3 34.1 %fusion.64 = f32[8,512,512]{2,1,0:T(8,128)S(1)} fusion(f32[8,512,512]{2,1,0:T(8,128)S(1)} %fusion.66, f32[512]{0:T(512)S(1)} %get-tuple-element.49, f32[512]{0:T(512)S(1)} %get-tuple-element.50), kind=kOutput, calls=%fused_computation.115 | convolution fusion | flops 12885688320 | bytes 16781312 | tf_op jit(solution)/shard_map/lj,tkj->tkl/dot_general | solution.py:100
  680.2 23.2 %convolution_bitcast_fusion.1 = f32[512,512,8]{0,1,2:T(8,128)} fusion(f32[8,512,512]{1,2,0:T(8,128)S(1)} %fusion.72, f32[512]{0:T(512)S(1)} %get-tuple-element.49, f32[512]{0:T(512)S(1)} %get-tuple-element.50), kind=kOutput, calls=%fused_computation.144 | convolution fusion | flops 12885688320 | bytes 16781312 | tf_op jit(solution)/shard_map/ki,tkj->tij/dot_general | solution.py:103
  713.9 184.9 %all_to_all.139 = f32[512,512,8]{1,2,0:T(8,128)S(1)} all-to-all(f32[512,512,8]{1,2,0:T(8,128)} %copy.207), channel_id=1, replica_groups=mesh['gx'=4,'gy'=8] {'gx'}, dimensions={0} | all-to-all | bytes 16777216 | tf_op jit(solution)/shard_map/all_to_all | solution.py:188
  919.2 94.1 %all-to-all-done.3 = f32[128,512,32]{0,2,1:T(8,128)} async-done(((f32[128,512,32]{0,2,1:T(8,128)}), f32[128,512,32]{0,2,1:T(8,128)}, u32[]{:S(2)}, u32[]{:S(2)}) %all-to-all-start.3) | async-done | bytes 8388640 | tf_op jit(solution)/shard_map/all_to_all | solution.py:187
  1069.4 36.8 %multiply_reduce_fusion.2 = (f32[]{:T(128)}, f32[]{:T(128)}, f32[128,64,256]{2,0,1:T(8,128)}) fusion(f32[128,64,256]{2,1,0:T(8,128)} %bitcast.97, f32[128,64,256]{2,0,1:T(8,128)} %fusion.59, f32[128,64,256]{2,0,1:T(8,128)} %copy-done.7, f32[1,64,256]{2,0,1:T(1,128)S(1)} %copy.214, f32[1,64,256]{2,0,1:T(1,128)S(1)} %copy.216, ...), kind=kLoop, calls=%fused_computation.131 | loop fusion | flops 52428800 | bytes 67506184 | tf_op jit(solution)/shard_map/reduce_sum | solution.py:136
  1106.2 41.2 %all-reduce.5 = (f32[]{:T(128)}, f32[]{:T(128)}) all-reduce(f32[]{:T(128)} %get-tuple-element.15, f32[]{:T(128)} %get-tuple-element.14), channel_id=1, replica_groups=mesh['gx'=4,'gy'=8] {'gx','gy'}, use_global_device_ids=true, to_apply=%region_1.2 | all-reduce | flops 2 | bytes 16 | tf_op jit(solution)/shard_map/psum | solution.py:125
  1169.1 186.9 %all_to_all.140 = f32[128,64,256]{0,1,2:T(8,128)S(1)} all-to-all(f32[128,64,256]{0,1,2:T(8,128)} %copy.226), channel_id=1, replica_groups=mesh['gx'=4,'gy'=8] {'gx'}, dimensions={2} | all-to-all | bytes 16777216 | tf_op jit(solution)/shard_map/all_to_all | solution.py:180
  1357.0 97.9 %all_to_all.141 = f32[512,64,64]{0,1,2:T(8,128)} all-to-all(f32[512,64,64]{0,1,2:T(8,128)S(1)} %bitcast.109), channel_id=1, replica_groups=mesh['gx'=4,'gy'=8] {'gy'}, dimensions={2} | all-to-all | bytes 16777216 | tf_op jit(solution)/shard_map/all_to_all | solution.py:179
  1463.1 22.6 %fusion.62 = f32[8,512,512]{2,1,0:T(8,128)S(1)} fusion(f32[512,512,8]{0,2,1:T(8,128)S(1)} %bitcast.103, f32[512]{0:T(512)S(1)} %get-tuple-element.49, f32[512]{0:T(512)S(1)} %get-tuple-element.50), kind=kOutput, calls=%fused_computation.113 | convolution fusion | flops 12885688320 | bytes 16781312 | tf_op jit(solution)/shard_map/ki,tij->tkj/dot_general | solution.py:99
  1485.7 34.1 %fusion.60 = f32[8,512,512]{2,1,0:T(8,128)S(1)} fusion(f32[8,512,512]{2,1,0:T(8,128)S(1)} %fusion.62, f32[512]{0:T(512)S(1)} %get-tuple-element.49, f32[512]{0:T(512)S(1)} %get-tuple-element.50), kind=kOutput, calls=%fused_computation.111 | convolution fusion | flops 12885688320 | bytes 16781312 | tf_op jit(solution)/shard_map/lj,tkj->tkl/dot_general | solution.py:100
  1539.6 23.2 %convolution_bitcast_fusion = f32[512,512,8]{0,1,2:T(8,128)} fusion(f32[8,512,512]{1,2,0:T(8,128)S(1)} %fusion.70, f32[512]{0:T(512)S(1)} %get-tuple-element.49, f32[512]{0:T(512)S(1)} %get-tuple-element.50), kind=kOutput, calls=%fused_computation.143 | convolution fusion | flops 12885688320 | bytes 16781312 | tf_op jit(solution)/shard_map/ki,tkj->tij/dot_general | solution.py:103
  1573.3 187.0 %all_to_all.142 = f32[512,512,8]{1,2,0:T(8,128)S(1)} all-to-all(f32[512,512,8]{1,2,0:T(8,128)} %copy.235), channel_id=1, replica_groups=mesh['gx'=4,'gy'=8] {'gx'}, dimensions={0} | all-to-all | bytes 16777216 | tf_op jit(solution)/shard_map/all_to_all | solution.py:188
  1775.5 97.8 %all_to_all.143 = f32[128,512,32]{0,2,1:T(8,128)S(1)} all-to-all(f32[128,512,32]{0,2,1:T(8,128)} %copy.237), channel_id=1, replica_groups=mesh['gx'=4,'gy'=8] {'gy'}, dimensions={1} | all-to-all | bytes 16777216 | tf_op jit(solution)/shard_map/all_to_all | solution.py:187
  1894.3 38.5 %psum.30 = f32[]{:T(128)} all-reduce(f32[]{:T(128)} %get-tuple-element.43), channel_id=1, replica_groups=mesh['gx'=4,'gy'=8] {'gx','gy'}, use_global_device_ids=true, to_apply=%region_5.6 | all-reduce | flops 1 | bytes 8 | tf_op jit(solution)/shard_map/psum | solution.py:125
  1964.1 20.2 multiply_reduce_fusion
  1984.3 45.3 %psum.31 = f32[]{:T(128)} all-reduce(f32[]{:T(128)} %get-tuple-element.18), channel_id=1, replica_groups=mesh['gx'=4,'gy'=8] {'gx','gy'}, use_global_device_ids=true, to_apply=%region_7.8 | all-reduce | flops 1 | bytes 8 | tf_op jit(solution)/shard_map/psum | solution.py:136
  (118 shorter events, 417.7 us)
Async XLA Ops:
  12.4 10.5 collective-permute-start
  17.3 9.7 collective-permute-start.1
  18.7 16.2 copy-start.6
  28.2 3.8 collective-permute-start.2
  29.5 5.4 collective-permute-start.3
  130.3 14.9 copy-start
  179.6 14.9 copy-start.1
  179.6 20.3 slice-start
  179.6 20.3 slice-start.1
  179.6 21.7 %slice-start.3 = ((s8[9469952]{0:T(1024)(128)(4,1)}), s8[4194304]{0:T(1024)(128)(4,1)S(1)}, s32[]{:S(2)}) async-start(s8[9469952]{0:T(1024)(128)(4,1)} %bitcast.94), calls=%async_computation.11 | async-start | bytes 8388608
  179.6 22.9 %slice-start.4 = ((s8[9469952]{0:T(1024)(128)(4,1)}), s8[4194304]{0:T(1024)(128)(4,1)S(1)}, s32[]{:S(2)}) async-start(s8[9469952]{0:T(1024)(128)(4,1)} %bitcast.94), calls=%async_computation.12 | async-start | bytes 8388608
  203.3 45.0 %copy-start.9 = (f32[66]{0:T(128)S(1)}, f32[66]{0:T(128)}, u32[]{:S(2)}) copy-start(f32[66]{0:T(128)} %and_convert_fusion) | copy-start | bytes 796
  490.0 105.6 %all-to-all-start.1 = ((f32[512,64,64]{0,1,2:T(8,128)}), f32[512,64,64]{0,1,2:T(8,128)}, u32[]{:S(2)}, u32[]{:S(2)}) async-start(f32[512,64,64]{0,1,2:T(8,128)} %bitcast.104), calls=%async_computation.1 | async-start | bytes 16777216 | tf_op jit(solution)/shard_map/all_to_all | solution.py:179
  914.3 99.0 %all-to-all-start.3 = ((f32[128,512,32]{0,2,1:T(8,128)}), f32[128,512,32]{0,2,1:T(8,128)}, u32[]{:S(2)}, u32[]{:S(2)}) async-start(f32[128,512,32]{0,2,1:T(8,128)} %copy.209), calls=%async_computation.3 | async-start | bytes 16777216 | tf_op jit(solution)/shard_map/all_to_all | solution.py:187
  1049.7 11.1 collective-permute-start.4
  1051.0 9.9 collective-permute-start.5
  1064.1 4.3 collective-permute-start.6
  1065.4 4.0 collective-permute-start.7
  1948.3 15.8 copy-start.4
  1949.8 6.4 collective-permute-start.8
  1951.3 6.4 collective-permute-start.9
  1958.8 4.3 collective-permute-start.10
  1960.1 4.0 collective-permute-start.11
  2056.7 12.0 copy-start.8
  (8 other events, 50.9 us)
where the time goes:
time: 2080 us
  blocking collectives  1060 us (51%)
  other arithmetic  354 us (17%)
  matrix products  223 us (11%)
  waiting for transfers between devices  203 us (10%)
  local copies, waits for them, and re-layouts  180 us (9%)
  starting transfers between devices  46.8 us (2%)
    all_to_all x2, blocking collectives, precondition(): lax.all_to_all(field, 'gx', split_axis=2, concat_axis=0, tiled=True)  372 us
    all_to_all x2, blocking collectives, precondition(): lax.all_to_all(hat, 'gx', split_axis=0, concat_axis=2, tiled=True)  372 us
    all_to_all x1, blocking collectives, precondition(): lax.all_to_all(lax.all_to_all(field, 'gx', split_axis=2, concat_axis=0, t...  97.9 us
    all_to_all x1, blocking collectives, precondition(): lax.all_to_all(lax.all_to_all(hat, 'gx', split_axis=0, concat_axis=2, til...  97.8 us
    mul x6, other arithmetic, smooth_axis(): 0.25 * (cut(field, 0, length - 2, axis) + 2.0 * cut(field, 1, length - 1,...  96.6 us
    all_to_all x1, waiting for transfers between devices, precondition(): lax.all_to_all(lax.all_to_all(hat, 'gx', split_axis=0, concat_axis=2, til...  94.1 us
    all_to_all x1, waiting for transfers between devices, precondition(): lax.all_to_all(lax.all_to_all(field, 'gx', split_axis=2, concat_axis=0, t...  94 us
    psum x2, blocking collectives, inner(): return lax.psum(jnp.sum(first * second), ('gx', 'gy'))  79.7 us
  transfers between devices with their start and end apart: 14, of which 9 were waited for; matrix products, arithmetic and copies ran while one was open for 0% of the time, Pallas kernels for 0%

commit v1 on v0

--- a/solution.py
+++ b/solution.py
@@ -176,13 +176,19 @@
     prior_y = weight_y[1:-1, :-2]
 
     def precondition(field):
-        whole = lax.all_to_all(
-            lax.all_to_all(field, "gx", split_axis=2, concat_axis=0, tiled=True),
-            "gy",
-            split_axis=2,
-            concat_axis=1,
-            tiled=True,
-        )
+        x = lax.all_to_all(field, "gx", split_axis=2, concat_axis=0, tiled=True)
+        ways, here = (lax.axis_size("gy"), lax.axis_index("gy"))
+        width_2 = x.shape[2] // ways
+        dims = list(x.shape)
+        dims[2] = width_2
+        height = dims[1]
+        dims[1] = height * ways
+        whole = jnp.zeros(dims, x.dtype)
+        for mask_2 in range(ways):
+            part = lax.dynamic_slice_in_dim(x, (here ^ mask_2) * width_2, width_2, axis=2)
+            if mask_2:
+                part = lax.ppermute(part, "gy", [(d, d ^ mask_2) for d in range(ways)])
+            whole = lax.dynamic_update_slice_in_dim(whole, part, (here ^ mask_2) * height, axis=1)
         hat = slice_solve(whole, table_x, table_y, plane_denom)
         back = lax.all_to_all(
             lax.all_to_all(hat, "gx", split_axis=0, concat_axis=2, tiled=True),

time: 2080 us -> 2120 us (1.019)
  blocking collectives: 1060 us -> 791 us
  waiting for transfers between devices: 203 us -> 457 us
  local copies, waits for them, and re-layouts: 180 us -> 228 us
    all_to_all x3 -> x1, blocking collectives: 470 us -> 190 us  [precondition(): x = lax.all_to_all(field, 'gx', split_axis=2, concat_axis=0, tiled=True)]
    ppermute x0 -> x14, waiting for transfers between devices: none -> 165 us  [precondition(): part = lax.ppermute(part, 'gy', [(d, d ^ mask_2) for d in range(ways)])]
    all_to_all x1, waiting for transfers between devices: 94 us -> 183 us  [precondition(): x = lax.all_to_all(field, 'gx', split_axis=2, concat_axis=0, tiled=True)]
    all_to_all x4, local copies, waits for them, and re-layouts: 21.8 us -> 45.5 us  [precondition(): x = lax.all_to_all(field, 'gx', split_axis=2, concat_axis=0, tiled=True)]
    unnamed x39 -> x43, local copies, waits for them, and re-layouts: 45.5 us -> 44.5 us
  transfers between devices with their start and end apart: 14 -> 28, of which waited for: 9 -> 15; matrix products, arithmetic and copies ran while one was open for 0% -> 1% of each run, Pallas kernels for 0% -> 0%
where the time goes in v1:
time: 2120 us; the launch traced here: 2110 us
  blocking collectives  791 us (37%)
  waiting for transfers between devices  457 us (22%)
  other arithmetic  355 us (17%)
  local copies, waits for them, and re-layouts  228 us (11%)
  matrix products  216 us (10%)
  starting transfers between devices  59.8 us (3%)
    all_to_all x2, blocking collectives, precondition(): lax.all_to_all(hat, 'gx', split_axis=0, concat_axis=2, tiled=True)  377 us
    all_to_all x1, blocking collectives, precondition(): x = lax.all_to_all(field, 'gx', split_axis=2, concat_axis=0, tiled=True)  190 us
    all_to_all x1, waiting for transfers between devices, precondition(): x = lax.all_to_all(field, 'gx', split_axis=2, concat_axis=0, tiled=True)  183 us
    ppermute x14, waiting for transfers between devices, precondition(): part = lax.ppermute(part, 'gy', [(d, d ^ mask_2) for d in range(ways)])  165 us
    all_to_all x1, blocking collectives, precondition(): lax.all_to_all(lax.all_to_all(hat, 'gx', split_axis=0, concat_axis=2, til...  98.1 us
    mul x6, other arithmetic, smooth_axis(): 0.25 * (cut(field, 0, length - 2, axis) + 2.0 * cut(field, 1, length - 1,...  96.8 us
    all_to_all x1, waiting for transfers between devices, precondition(): lax.all_to_all(lax.all_to_all(hat, 'gx', split_axis=0, concat_axis=2, til...  94.1 us
    psum x2, blocking collectives, inner(): return lax.psum(jnp.sum(first * second), ('gx', 'gy'))  80.1 us
  transfers between devices with their start and end apart: 28, of which 15 were waited for; matrix products, arithmetic and copies ran while one was open for 1% of the time, Pallas kernels for 0%

profile of v1, /device:TPU:0, one launch (start us, length us, event | category | flops | bytes accessed | tf_op | source)
XLA Modules:
  0.0 2111.4 jit_solution(2778839904464890453)
XLA Ops:
  47.0 53.7 %fusion.75 = (f32[132,68,256]{2,0,1:T(8,128)}, f32[132,68,256]{2,0,1:T(8,128)}, f32[132,68,256]{2,0,1:T(8,128)}, f32[132,68,256]{2,0,1:T(8,128)}) fusion(f32[132,68]{0,1:T(8,128)S(1)} %multiply_multiply_fusion, f32[134,70,256]{2,0,1:T(8,128)} %copy-done.2, f32[132,68,256]{2,0,1:T(8,128)} %slice.298), kind=kLoop, calls=%fused_computation.142 | loop fusion | flops 36765696 | bytes 82758720 | tf_op jit(solution)/shard_map/mul | solution.py:55
  100.7 29.4 %fusion.6 = (f32[130,68,256]{2,0,1:T(8,128)}, f32[130,68,256]{2,0,1:T(8,128)}) fusion(f32[132,68,256]{2,0,1:T(8,128)} %get-tuple-element.29, f32[132,68,256]{2,0,1:T(8,128)} %get-tuple-element.30), kind=kLoop, calls=%fused_computation.23 | loop fusion | flops 18104320 | bytes 72417280 | tf_op jit(solution)/shard_map/mul | solution.py:33
  150.0 29.6 %fusion.2 = (f32[130,68,256]{2,0,1:T(8,128)}, f32[130,68,256]{2,0,1:T(8,128)}) fusion(f32[132,68,256]{2,0,1:T(8,128)} %get-tuple-element.27, f32[132,68,256]{2,0,1:T(8,128)} %get-tuple-element.28), kind=kLoop, calls=%fused_computation.15 | loop fusion | flops 18104320 | bytes 72417280 | tf_op jit(solution)/shard_map/mul | solution.py:33
  203.3 45.1 %fusion.24 = (f32[130,66,256]{2,0,1:T(8,128)}, f32[130,66,256]{2,0,1:T(8,128)}, f32[130,66,256]{2,0,1:T(8,128)}, f32[130,66,256]{2,0,1:T(8,128)}) fusion(f32[130,66,256]{2,0,1:T(8,128)} %broadcast_multiply_fusion.3, f32[130,68,256]{2,0,1:T(8,128)} %get-tuple-element.62, f32[130]{0:T(256)S(1)} %and_convert_fusion.1, f32[130,68,256]{2,0,1:T(8,128)S(1)} %bitcast.81, ...), kind=kLoop, calls=%fused_computation.47 | loop fusion | flops 61501440 | bytes 140575232 | tf_op jit(solution)/shard_map/mul | solution.py:170
  248.4 27.0 %fusion.30 = (f32[130,66,256]{2,0,1:T(8,128)}, f32[130,66,256]{2,0,1:T(8,128)}) fusion(f32[130,66,256]{2,0,1:T(8,128)} %get-tuple-element.24, f32[130,66,256]{2,0,1:T(8,128)} %broadcast_multiply_fusion.2, f32[130,68,256]{2,0,1:T(8,128)} %get-tuple-element.61, f32[130,66,256]{2,0,1:T(8,128)} %get-tuple-element.23, f32[66]{0:T(128)S(1)} %copy-done.11), kind=kLoop, calls=%fused_computation.53 | loop fusion | flops 24161280 | bytes 70287624 | tf_op jit(solution)/shard_map/mul | solution.py:171
  306.2 183.4 %all-to-all-done = f32[128,64,256]{0,1,2:T(8,128)} async-done(((f32[128,64,256]{0,1,2:T(8,128)}), f32[128,64,256]{0,1,2:T(8,128)}, u32[]{:S(2)}, u32[]{:S(2)}) %all-to-all-start) | async-done | bytes 8388640 | tf_op jit(solution)/shard_map/all_to_all | solution.py:179
  553.7 20.0 collective-permute-done.6
  575.1 44.5 %collective-permute-done.8 = f32[512,64,8]{0,2,1:T(8,128)S(1)} collective-permute-done((f32[512,64,8]{0,2,1:T(8,128)}, f32[512,64,8]{0,2,1:T(8,128)S(1)}, u32[]{:S(2)}, u32[]{:S(2)}) %collective-permute-start.8) | collective-permute-done | bytes 1048608 | tf_op jit(solution)/shard_map/ppermute | solution.py:190
  640.3 34.1 %fusion.64 = f32[8,512,512]{2,1,0:T(8,128)S(1)} fusion(f32[8,512,512]{2,1,0:T(8,128)S(1)} %fusion.66, f32[512]{0:T(512)S(1)} %get-tuple-element.65, f32[512]{0:T(512)S(1)} %get-tuple-element.66), kind=kOutput, calls=%fused_computation.113 | convolution fusion | flops 12885688320 | bytes 16781312 | tf_op jit(solution)/shard_map/lj,tkj->tkl/dot_general | solution.py:100
  694.2 23.4 %convolution_bitcast_fusion.1 = f32[512,512,8]{0,1,2:T(8,128)} fusion(f32[8,512,512]{1,2,0:T(8,128)S(1)} %fusion.70, f32[512]{0:T(512)S(1)} %get-tuple-element.65, f32[512]{0:T(512)S(1)} %get-tuple-element.66), kind=kOutput, calls=%fused_computation.140 | convolution fusion | flops 12885688320 | bytes 16781312 | tf_op jit(solution)/shard_map/ki,tkj->tij/dot_general | solution.py:103
  728.1 188.4 %all_to_all.102 = f32[512,512,8]{1,2,0:T(8,128)S(1)} all-to-all(f32[512,512,8]{1,2,0:T(8,128)} %copy.237), channel_id=1, replica_groups=mesh['gx'=4,'gy'=8] {'gx'}, dimensions={0} | all-to-all | bytes 16777216 | tf_op jit(solution)/shard_map/all_to_all | solution.py:194
  937.0 94.1 %all-to-all-done.2 = f32[128,512,32]{0,2,1:T(8,128)} async-done(((f32[128,512,32]{0,2,1:T(8,128)}), f32[128,512,32]{0,2,1:T(8,128)}, u32[]{:S(2)}, u32[]{:S(2)}) %all-to-all-start.2) | async-done | bytes 8388640 | tf_op jit(solution)/shard_map/all_to_all | solution.py:193
  1087.1 36.8 %multiply_reduce_fusion.2 = (f32[]{:T(128)}, f32[]{:T(128)}, f32[128,64,256]{2,0,1:T(8,128)}) fusion(f32[128,64,256]{2,1,0:T(8,128)} %bitcast.85, f32[128,64,256]{2,0,1:T(8,128)} %fusion.59, f32[128,64,256]{2,0,1:T(8,128)} %copy-done.7, f32[1,64,256]{2,0,1:T(1,128)S(1)} %copy.244, f32[1,64,256]{2,0,1:T(1,128)S(1)} %copy.246, ...), kind=kLoop, calls=%fused_computation.127 | loop fusion | flops 52428800 | bytes 67506184 | tf_op jit(solution)/shard_map/reduce_sum | solution.py:136
  1123.9 41.7 %all-reduce.5 = (f32[]{:T(128)}, f32[]{:T(128)}) all-reduce(f32[]{:T(128)} %get-tuple-element.15, f32[]{:T(128)} %get-tuple-element.14), channel_id=1, replica_groups=mesh['gx'=4,'gy'=8] {'gx','gy'}, use_global_device_ids=true, to_apply=%region_1.2 | all-reduce | flops 2 | bytes 16 | tf_op jit(solution)/shard_map/psum | solution.py:125
  1187.1 190.2 %all_to_all.103 = f32[128,64,256]{0,1,2:T(8,128)} all-to-all(f32[128,64,256]{0,1,2:T(8,128)} %copy.256), channel_id=1, replica_groups=mesh['gx'=4,'gy'=8] {'gx'}, dimensions={2} | all-to-all | bytes 16777216 | tf_op jit(solution)/shard_map/all_to_all | solution.py:179
  1432.5 20.7 collective-permute-done.17
  1454.5 44.8 %collective-permute-done.19 = f32[512,64,8]{0,2,1:T(8,128)S(1)} collective-permute-done((f32[512,64,8]{0,2,1:T(8,128)S(1)}, f32[512,64,8]{0,2,1:T(8,128)S(1)}, u32[]{:S(2)}, u32[]{:S(2)}) %collective-permute-start.19) | collective-permute-done | bytes 1048608 | tf_op jit(solution)/shard_map/ppermute | solution.py:190
  1520.2 34.1 %fusion.60 = f32[8,512,512]{2,1,0:T(8,128)S(1)} fusion(f32[8,512,512]{2,1,0:T(8,128)S(1)} %fusion.62, f32[512]{0:T(512)S(1)} %get-tuple-element.65, f32[512]{0:T(512)S(1)} %get-tuple-element.66), kind=kOutput, calls=%fused_computation.109 | convolution fusion | flops 12885688320 | bytes 16781312 | tf_op jit(solution)/shard_map/lj,tkj->tkl/dot_general | solution.py:100
  1574.1 23.2 %convolution_bitcast_fusion = f32[512,512,8]{0,1,2:T(8,128)} fusion(f32[8,512,512]{1,2,0:T(8,128)S(1)} %fusion.68, f32[512]{0:T(512)S(1)} %get-tuple-element.65, f32[512]{0:T(512)S(1)} %get-tuple-element.66), kind=kOutput, calls=%fused_computation.139 | convolution fusion | flops 12885688320 | bytes 16781312 | tf_op jit(solution)/shard_map/ki,tkj->tij/dot_general | solution.py:103
  1607.7 188.4 %all_to_all.104 = f32[512,512,8]{1,2,0:T(8,128)S(1)} all-to-all(f32[512,512,8]{1,2,0:T(8,128)} %copy.269), channel_id=1, replica_groups=mesh['gx'=4,'gy'=8] {'gx'}, dimensions={0} | all-to-all | bytes 16777216 | tf_op jit(solution)/shard_map/all_to_all | solution.py:194
  1811.4 98.1 %all_to_all.105 = f32[128,512,32]{0,2,1:T(8,128)S(1)} all-to-all(f32[128,512,32]{0,2,1:T(8,128)} %copy.271), channel_id=1, replica_groups=mesh['gx'=4,'gy'=8] {'gy'}, dimensions={1} | all-to-all | bytes 16777216 | tf_op jit(solution)/shard_map/all_to_all | solution.py:193
  1928.4 38.5 %psum.30 = f32[]{:T(128)} all-reduce(f32[]{:T(128)} %get-tuple-element.59), channel_id=1, replica_groups=mesh['gx'=4,'gy'=8] {'gx','gy'}, use_global_device_ids=true, to_apply=%region_5.6 | all-reduce | flops 1 | bytes 8 | tf_op jit(solution)/shard_map/psum | solution.py:125
  1998.2 20.2 multiply_reduce_fusion
  2018.4 45.3 %psum.31 = f32[]{:T(128)} all-reduce(f32[]{:T(128)} %get-tuple-element.18), channel_id=1, replica_groups=mesh['gx'=4,'gy'=8] {'gx','gy'}, use_global_device_ids=true, to_apply=%region_7.8 | all-reduce | flops 1 | bytes 8 | tf_op jit(solution)/shard_map/psum | solution.py:136
  (168 shorter events, 551.3 us)
Async XLA Ops:
  12.4 10.5 collective-permute-start
  17.3 9.7 collective-permute-start.1
  29.5 5.4 collective-permute-start.3
  300.5 189.1 %all-to-all-start = ((f32[128,64,256]{0,1,2:T(8,128)}), f32[128,64,256]{0,1,2:T(8,128)}, u32[]{:S(2)}, u32[]{:S(2)}) async-start(f32[128,64,256]{0,1,2:T(8,128)} %copy.224), calls=%async_computation | async-start | bytes 16777216 | tf_op jit(solution)/shard_map/all_to_all | solution.py:179
  518.8 12.1 collective-permute-start.4
  519.7 31.9 %collective-permute-start.5 = (f32[512,64,8]{0,2,1:T(8,128)}, f32[512,64,8]{0,2,1:T(8,128)}, u32[]{:S(2)}, u32[]{:S(2)}) collective-permute-start(f32[512,64,8]{0,2,1:T(8,128)} %get-tuple-element.54), channel_id=1, source_target_pairs={{0,2},{1,3},{2,0},{3,1},{4,6},{5,7},{6,4},{7,5},{8,10},{9,11},{10,... | collective-permute-start | bytes 3145736 | tf_op jit(solution)/shard_map/ppermute | solution.py:190
  527.4 46.3 %collective-permute-start.6 = (f32[512,64,8]{0,2,1:T(8,128)}, f32[512,64,8]{0,2,1:T(8,128)S(1)}, u32[]{:S(2)}, u32[]{:S(2)}) collective-permute-start(f32[512,64,8]{0,2,1:T(8,128)} %get-tuple-element.53), channel_id=1, source_target_pairs={{0,3},{1,2},{2,1},{3,0},{4,7},{5,6},{6,5},{7,4},{8,11},{9,10},{10,... | collective-permute-start | bytes 3145736 | tf_op jit(solution)/shard_map/ppermute | solution.py:190
  527.6 46.7 %collective-permute-start.7 = (f32[512,64,8]{0,2,1:T(8,128)}, f32[512,64,8]{0,2,1:T(8,128)S(1)}, u32[]{:S(2)}, u32[]{:S(2)}) collective-permute-start(f32[512,64,8]{0,2,1:T(8,128)} %get-tuple-element.52), channel_id=1, source_target_pairs={{0,4},{1,5},{2,6},{3,7},{4,0},{5,1},{6,2},{7,3},{8,12},{9,13},{10,... | collective-permute-start | bytes 3145736 | tf_op jit(solution)/shard_map/ppermute | solution.py:190
  528.8 90.8 %collective-permute-start.8 = (f32[512,64,8]{0,2,1:T(8,128)}, f32[512,64,8]{0,2,1:T(8,128)S(1)}, u32[]{:S(2)}, u32[]{:S(2)}) collective-permute-start(f32[512,64,8]{0,2,1:T(8,128)} %get-tuple-element.51), channel_id=1, source_target_pairs={{0,5},{1,4},{2,7},{3,6},{4,1},{5,0},{6,3},{7,2},{8,13},{9,12},{10,... | collective-permute-start | bytes 3145736 | tf_op jit(solution)/shard_map/ppermute | solution.py:190
  530.9 89.4 %collective-permute-start.9 = (f32[512,64,8]{0,2,1:T(8,128)S(1)}, f32[512,64,8]{0,2,1:T(8,128)S(1)}, u32[]{:S(2)}, u32[]{:S(2)}) collective-permute-start(f32[512,64,8]{0,2,1:T(8,128)S(1)} %get-tuple-element.50), channel_id=1, source_target_pairs={{0,6},{1,7},{2,4},{3,5},{4,2},{5,3},{6,0},{7,1},{8,14},{9,15},{10,... | collective-permute-start | bytes 3145736 | tf_op jit(solution)/shard_map/ppermute | solution.py:190
  551.6 69.4 %collective-permute-start.10 = (f32[512,64,8]{0,2,1:T(8,128)S(1)}, f32[512,64,8]{0,2,1:T(8,128)S(1)}, u32[]{:S(2)}, u32[]{:S(2)}) collective-permute-start(f32[512,64,8]{0,2,1:T(8,128)S(1)} %get-tuple-element.49), channel_id=1, source_target_pairs={{0,7},{1,6},{2,5},{3,4},{4,3},{5,2},{6,1},{7,0},{8,15},{9,14},{10,... | collective-permute-start | bytes 3145736 | tf_op jit(solution)/shard_map/ppermute | solution.py:190
  932.0 99.0 %all-to-all-start.2 = ((f32[128,512,32]{0,2,1:T(8,128)}), f32[128,512,32]{0,2,1:T(8,128)}, u32[]{:S(2)}, u32[]{:S(2)}) async-start(f32[128,512,32]{0,2,1:T(8,128)} %copy.239), calls=%async_computation.2 | async-start | bytes 16777216 | tf_op jit(solution)/shard_map/all_to_all | solution.py:193
  1067.5 11.0 collective-permute-start.11
  1068.8 9.7 collective-permute-start.12
  1081.7 4.3 collective-permute-start.13
  1404.3 6.5 collective-permute-start.15
  1404.4 26.8 %collective-permute-start.16 = (f32[512,64,8]{0,2,1:T(8,128)S(1)}, f32[512,64,8]{0,2,1:T(8,128)S(1)}, u32[]{:S(2)}, u32[]{:S(2)}) collective-permute-start(f32[512,64,8]{0,2,1:T(8,128)S(1)} %get-tuple-element.44), channel_id=1, source_target_pairs={{0,2},{1,3},{2,0},{3,1},{4,6},{5,7},{6,4},{7,5},{8,10},{9,11},{10,... | collective-permute-start | bytes 3145736 | tf_op jit(solution)/shard_map/ppermute | solution.py:190
  1407.2 46.0 %collective-permute-start.17 = (f32[512,64,8]{0,2,1:T(8,128)S(1)}, f32[512,64,8]{0,2,1:T(8,128)S(1)}, u32[]{:S(2)}, u32[]{:S(2)}) collective-permute-start(f32[512,64,8]{0,2,1:T(8,128)S(1)} %get-tuple-element.43), channel_id=1, source_target_pairs={{0,3},{1,2},{2,1},{3,0},{4,7},{5,6},{6,5},{7,4},{8,11},{9,10},{10,... | collective-permute-start | bytes 3145736 | tf_op jit(solution)/shard_map/ppermute | solution.py:190
  1407.2 46.6 %collective-permute-start.18 = (f32[512,64,8]{0,2,1:T(8,128)S(1)}, f32[512,64,8]{0,2,1:T(8,128)S(1)}, u32[]{:S(2)}, u32[]{:S(2)}) collective-permute-start(f32[512,64,8]{0,2,1:T(8,128)S(1)} %get-tuple-element.42), channel_id=1, source_target_pairs={{0,4},{1,5},{2,6},{3,7},{4,0},{5,1},{6,2},{7,3},{8,12},{9,13},{10,... | collective-permute-start | bytes 3145736 | tf_op jit(solution)/shard_map/ppermute | solution.py:190
  1409.0 90.3 %collective-permute-start.19 = (f32[512,64,8]{0,2,1:T(8,128)S(1)}, f32[512,64,8]{0,2,1:T(8,128)S(1)}, u32[]{:S(2)}, u32[]{:S(2)}) collective-permute-start(f32[512,64,8]{0,2,1:T(8,128)S(1)} %get-tuple-element.41), channel_id=1, source_target_pairs={{0,5},{1,4},{2,7},{3,6},{4,1},{5,0},{6,3},{7,2},{8,13},{9,12},{10,... | collective-permute-start | bytes 3145736 | tf_op jit(solution)/shard_map/ppermute | solution.py:190
  1410.8 89.2 %collective-permute-start.20 = (f32[512,64,8]{0,2,1:T(8,128)S(1)}, f32[512,64,8]{0,2,1:T(8,128)S(1)}, u32[]{:S(2)}, u32[]{:S(2)}) collective-permute-start(f32[512,64,8]{0,2,1:T(8,128)S(1)} %get-tuple-element.40), channel_id=1, source_target_pairs={{0,6},{1,7},{2,4},{3,5},{4,2},{5,3},{6,0},{7,1},{8,14},{9,15},{10,... | collective-permute-start | bytes 3145736 | tf_op jit(solution)/shard_map/ppermute | solution.py:190
  1431.2 69.5 %collective-permute-start.21 = (f32[512,64,8]{0,2,1:T(8,128)S(1)}, f32[512,64,8]{0,2,1:T(8,128)S(1)}, u32[]{:S(2)}, u32[]{:S(2)}) collective-permute-start(f32[512,64,8]{0,2,1:T(8,128)S(1)} %get-tuple-element.39), channel_id=1, source_target_pairs={{0,7},{1,6},{2,5},{3,4},{4,3},{5,2},{6,1},{7,0},{8,15},{9,14},{10,... | collective-permute-start | bytes 3145736 | tf_op jit(solution)/shard_map/ppermute | solution.py:190
  1983.9 6.4 collective-permute-start.22
  1985.5 6.4 collective-permute-start.23
  (24 other events, 546.8 us)
